TPU v7x, 256 devices: a whole 4x4x8 slice. The times are simulated.
256 devices in a mesh: dp: 32 (over z, y), ctx: 8 (over x, core).
Axes of the slice: x: 4, y: 4, z: 8, core: 2. Of those that a mesh axis runs over, the one named last changes fastest.
Arguments:
- uvqk: bfloat16 [32, 1024, 4096], P(None, 'ctx', 'dp'), may hold values from -1.5 to 1.5
- lengths: int32 [32], replicated, may hold values from 1 to 1024, as said below
- assignment: int32 [32], replicated, may hold values from 0 to 31, as said below
- buckets: int32 [1024], replicated, may hold values from 0 to 127
- rel_bias: float32 [8, 128], replicated, may hold values from -3 to 3
- cotangent: bfloat16 [32, 1024, 1024], P('dp', 'ctx'), may hold values from -6 to 6
Outputs:
- output: bfloat16 [32, 1024, 1024], P('dp', 'ctx')
- d_uvqk: bfloat16 [32, 1024, 4096], P(None, 'ctx', 'dp')
- d_bias: float32 [8, 128], replicated
Inputs may be any that keep to these rules, and one draw needn't show every extreme that they name: `lengths`: valid actions of each user; some user has exactly 1024. `assignment`: A permutation of the user ids. Slot d * 1 + t is the t-th slot of index d of dp; users are dealt to slots in order of falling length, alternating the direction over dp from one round to the next (with 1 = 1 there is a single round: slot d holds the user of rank d).
All inputs are finite; a program needn't handle non-finite values.
Results may differ from a plain program's by a relative error of at most 0.0055.
Values may be sent and summed in bfloat16 or wider, within the bound.
A program may use at most 128 MiB of HBM per device.

v0:
```python
import functools

import jax
import jax.numpy as jnp
from jax import lax
from jax.experimental import pallas as pl
from jax.experimental.pallas import tpu as pltpu
from jax.sharding import PartitionSpec as P

MESH = pl.DeviceIdType.MESH
Y = 4
TB = 256
W = 128
NN = (((1,), (0,)), ((), ()))
NT = (((1,), (1,)), ((), ()))


def mm(a, b, dims):
    return lax.dot_general(a, b, dims, preferred_element_type=jnp.float32)


def tile_at(ib, jb):
    return ib * (ib + 1) // 2 + jb


def ctx_of(h, p, H):
    if H != 8:
        return h
    y, b = lax.rem(h, 4), lax.div(h, 4)
    return lax.rem(y + 2 * b + lax.rem(p, 4), 4) * 2 + b


def head_of(c, p, H):
    if H != 8:
        return c
    x, b = lax.div(c, 2), lax.rem(c, 2)
    return b * 4 + lax.rem(x + 8 - 2 * b - lax.rem(p, 4), 4)


def kernel(
    H,
    U,
    assign_hbm,
    lengths_hbm,
    uvqk_hbm,
    cot_hbm,
    buckets_hbm,
    rel_hbm,
    out,
    grads,
    dbias,
    assign,
    lengths,
    uvqk,
    cot,
    buckets,
    rel,
    in_send,
    in_recv,
    cot_recv,
    out_send,
    g_send,
    toep,
    wts,
    dsl,
    diag,
    vt,
    kt,
    gt,
    at,
    dat,
    st_recv,
    st_send,
    db_send,
    db_recv,
    db_sum,
    db_mine,
    db_all,
    s_load,
    s_in,
    r_in,
    s_cot,
    r_cot,
    s_st,
    r_st,
    s_out,
    r_out,
    s_g,
    r_g,
    s_db,
    r_db,
    s_dbs,
    r_dbs,
    s_dba,
    r_dba,
):
    k = lax.axis_index("dp")
    c = lax.axis_index("ctx")
    e = lax.rem(k, H)
    comp = lax.div(k, H)
    head = head_of(c, k, H)
    own = e == head
    LEN = H * W
    nt = LEN // TB
    per = TB // W

    def rows(cc):
        if isinstance(cc, int):
            return pl.ds(cc * W, W)
        return pl.ds(pl.multiple_of(cc * W, W), W)

    def remote(src, dst, ss, rs, dev):
        return pltpu.make_async_remote_copy(
            src_ref=src, dst_ref=dst, send_sem=ss, recv_sem=rs, device_id=dev, device_id_type=MESH
        )

    def arrived(ref, ss, rs):
        remote(ref, ref, ss, rs, (k, c)).wait_recv()

    def loop(lo, hi, body):
        def step(i, _):
            body(i)
            return 0

        lax.fori_loop(lo, hi, step, 0)

    loads = [
        pltpu.make_async_copy(src, dst, s_load.at[n])
        for n, (src, dst) in enumerate(
            (
                (assign_hbm, assign),
                (uvqk_hbm, uvqk),
                (cot_hbm, cot),
                (lengths_hbm, lengths),
                (buckets_hbm, buckets),
                (rel_hbm, rel),
            )
        )
    ]
    for load in loads:
        load.start()
    barrier = pltpu.get_barrier_semaphore()

    for o in range(4 * H):
        far = (2, 3, 1, 0)[o // H]
        kk, cc = lax.rem(comp + far, 4) * H + head, lax.rem(c + o, H)
        if o % H or far:
            pl.semaphore_signal(barrier, inc=1, device_id=(kk, cc), device_id_type=MESH)
            continue

        @pl.when(kk != k)
        def _(kk=kk, cc=cc):
            pl.semaphore_signal(barrier, inc=1, device_id=(kk, cc), device_id_type=MESH)

    for o in range(1, H):
        pl.semaphore_signal(
            barrier, inc=1, device_id=(k, lax.rem(c + o, H)), device_id_type=MESH
        )

    for load in loads:
        load.wait()

    def arrange(p):
        in_send[p] = uvqk[assign[p]]

    loop(0, U, arrange)
    pl.semaphore_wait(barrier, U + H - 1 - own.astype(jnp.int32))

    z, y = lax.div(k, Y), lax.rem(k, Y)
    Z = U // Y

    def in_copy(o):
        dz, dy = (o // Y, o % Y) if isinstance(o, int) else (lax.div(o, Y), lax.rem(o, Y))
        p = lax.rem(z + dz, Z) * Y + lax.rem(y + dy, Y)
        return remote(
            in_send.at[p],
            in_recv.at[comp, rows(c)],
            s_in.at[o],
            r_in.at[comp * H + c],
            (p, ctx_of(e, p, H)),
        )

    @pl.when(jnp.logical_not(own))
    def _():
        in_copy(0).start()

    @pl.when(own)
    def _():
        pltpu.make_async_copy(
            in_send.at[k], in_recv.at[comp, rows(c)], r_in.at[comp * H + c]
        ).start()

    def cot_copy(o):
        cc = lax.rem(c + o, H)
        return remote(
            cot.at[:, rows(head_of(cc, k, H))],
            cot_recv.at[rows(c)],
            s_cot.at[o],
            r_cot.at[c],
            (k, cc),
        )

    ways = sorted(range(Z), key=lambda dz: dz)
    turn = [dz * Y + dy for dz in ways for dy in range(Y)]
    for n, o in enumerate(turn):
        if o > 0:
            in_copy(o).start()
        if n % Y == 1 and 0 < n // Y + 1 < H:
            cot_copy(n // Y + 1).start()
    for o in range(len(ways) + 1, H):
        cot_copy(o).start()
    cot_recv[rows(c), :] = cot[:, rows(head)]

    eye = lax.broadcasted_iota(jnp.int32, (W, W), 0) == lax.broadcasted_iota(
        jnp.int32, (W, W), 1
    )
    onehot = lax.broadcasted_iota(jnp.int32, (W, LEN), 0) == buckets[...]
    rel_col = jnp.sum(jnp.where(eye, rel[pl.ds(head, 1), :], 0.0), axis=1, keepdims=True)
    relative = jnp.sum(jnp.where(onehot, rel_col, 0.0), axis=0, keepdims=True)
    row8 = lax.broadcasted_iota(jnp.int32, (8, 2 * TB), 0)
    for m in range(nt):
        low = relative[:, m * TB : (m + 1) * TB]
        before = relative[:, (m - 1) * TB : m * TB] if m else low
        x = jnp.broadcast_to(jnp.concatenate([low, before], 1), (8, 2 * TB))
        for bit in (1, 2, 4):
            x = jnp.where((row8 & bit) != 0, pltpu.roll(x, bit, 1), x)
        size = 8
        while size < TB:
            x = jnp.concatenate([x, pltpu.roll(x, size, 1)], 0)
            size *= 2
        toep[m] = x[:, :TB]

    def come(which, cc):
        arrived(in_recv.at[which, rows(cc)], s_in.at[0], r_in.at[which * H + cc])

    def turned(which, cc):
        block = in_recv[which, cc * W : (cc + 1) * W].astype(jnp.float32)
        return block.T.astype(jnp.bfloat16)

    user_len = lengths[assign[k]]
    for which in (1, 2, 3):
        for cc in range(H):
            come(which, cc)
    for cc in range(H):
        vt[:, cc * W : (cc + 1) * W] = turned(1, cc)
    key_at = lax.broadcasted_iota(jnp.int32, (TB, TB), 0)
    for ib in range(nt):
        query_at = lax.broadcasted_iota(jnp.int32, (1, TB), 1) + ib * TB
        limit = jnp.where(query_at < user_len, query_at, -1)
        q = in_recv[2, ib * TB : (ib + 1) * TB]
        acc = jnp.zeros((W, TB), jnp.float32)
        for jb in range(ib + 1):
            t = tile_at(ib, jb)
            score = mm(in_recv[3, jb * TB : (jb + 1) * TB], q, NT) + toep[ib - jb]
            live = key_at <= limit - jb * TB
            sig = 0.5 + 0.5 * jnp.tanh(0.5 * score)
            weight = score * sig
            slope = sig + weight * (1.0 - sig)
            wb = jnp.where(live, weight, 0.0).astype(jnp.bfloat16)
            wts[t] = wb
            dsl[t] = jnp.where(live, slope, 0.0)
            acc = acc + mm(vt[:, jb * TB : (jb + 1) * TB], wb, NN)
        at[:, ib * TB : (ib + 1) * TB] = acc

    gsums = []
    for cc in range(H):
        blk = slice(cc * W, (cc + 1) * W)
        come(0, cc)

        @pl.when(c != cc)
        def _(cc=cc):
            arrived(cot_recv.at[rows(cc)], s_cot.at[0], r_cot.at[cc])

        grad = (cot_recv[blk].astype(jnp.float32) * in_recv[0, blk].astype(jnp.float32)).T
        gt[:, blk] = grad
        gsums.append(jnp.sum(grad, axis=0, keepdims=True))

    means, spreads, gdots = [], [], []
    for r in range(H):
        blk = slice(r * W, (r + 1) * W)
        a = at[:, blk]
        mean = jnp.sum(a, axis=0, keepdims=True) * (1.0 / W)
        centered = a - mean
        means.append(mean)
        spreads.append(jnp.sum(centered * centered, axis=0, keepdims=True))
        gdots.append(jnp.sum(gt[:, blk] * centered, axis=0, keepdims=True))
    for n, rows_of in enumerate((means, spreads, gsums, gdots)):
        st_send[n] = jnp.concatenate(rows_of, 0)

    def st_copy(o):
        cc = lax.rem(c + o, H)
        return remote(st_send, st_recv.at[c], s_st.at[o], r_st.at[c], (k, cc))

    loop(1, H, lambda o: st_copy(o).start())
    st_recv[c] = st_send[...]

    for cc in range(H):
        kt[:, cc * W : (cc + 1) * W] = turned(3, cc)

    def st_wait(o):
        cc = lax.rem(c + o, H)
        arrived(st_recv.at[cc], s_st.at[0], r_st.at[cc])

    loop(1, H, st_wait)

    D = H * W
    mean = st_recv[0, 0]
    for h in range(1, H):
        mean = mean + st_recv[h, 0]
    mean = mean * (1.0 / H)
    square = jnp.zeros_like(mean)
    g_total = jnp.zeros_like(mean)
    gn_total = jnp.zeros_like(mean)
    for h in range(H):
        off = st_recv[h, 0] - mean
        square = square + (st_recv[h, 1] + W * (off * off))
        g_total = g_total + st_recv[h, 2]
        gn_total = gn_total + (st_recv[h, 3] + off * st_recv[h, 2])
    inv = lax.rsqrt(square * (1.0 / D) + 1e-05)
    g_mean = g_total * (1.0 / D)
    gn_mean = gn_total * inv * (1.0 / D)
    for r in range(H):
        blk = slice(r * W, (r + 1) * W)
        row = slice(r, r + 1)
        normed = (at[:, blk] - mean[row]) * inv[row]
        dat[:, blk] = (
            (gt[:, blk] - g_mean[row] - normed * gn_mean[row]) * inv[row]
        ).astype(jnp.bfloat16)
        natural = normed.T
        out_send[blk] = (natural * in_recv[0, blk].astype(jnp.float32)).astype(jnp.bfloat16)
        g_send[0, blk] = (natural * cot_recv[blk].astype(jnp.float32)).astype(jnp.bfloat16)

    def g_copy(which, o):
        cc = lax.rem(c + o, H)
        return remote(
            g_send.at[which, rows(cc)],
            grads.at[k],
            s_g.at[which * H + o],
            r_g.at[k],
            (which * H + head, cc),
        )

    early = range(1, H // 2 + 1)

    def g_start(o):
        for n in range(4):
            which = lax.rem(comp + n, 4)
            copy = g_copy(which, o)
            if o in early:

                @pl.when(which != 0)
                def _(copy=copy):
                    copy.start()

                continue
            if o > 0:
                copy.start()
                continue
            mine = which * H + head == k

            @pl.when(jnp.logical_not(mine))
            def _(copy=copy):
                copy.start()

            @pl.when(mine)
            def _(which=which):
                pltpu.make_async_copy(g_send.at[which, rows(c)], grads.at[k], r_g.at[k]).start()

    def g_left(o):
        for which in range(4):
            if o > 0:
                g_copy(which, o).wait_send()
                continue

            @pl.when(which * H + head != k)
            def _(which=which):
                g_copy(which, 0).wait_send()

    def out_copy(o):
        cc = lax.rem(c + o, H)
        return remote(
            out_send.at[rows(cc)], out.at[:, rows(head)], s_out.at[o], r_out.at[c], (k, cc)
        )

    for o in early:
        g_copy(0, o).start()
        out_copy(o).start()
    keep = pltpu.make_async_copy(out_send.at[rows(c)], out.at[:, rows(head)], s_out.at[0])
    keep.start()

    q_acc = [jnp.zeros((W, TB), jnp.float32) for _ in range(nt)]
    for jb in range(nt):
        value = in_recv[1, jb * TB : (jb + 1) * TB]
        acc = jnp.zeros((TB, W), jnp.float32)
        for ib in range(jb, nt):
            t = tile_at(ib, jb)
            ds = mm(value, dat[:, ib * TB : (ib + 1) * TB], NN) * dsl[t]
            if jb == 0:
                diag[ib - jb] = ds
            else:
                diag[ib - jb] += ds
            dsb = ds.astype(jnp.bfloat16)
            acc = acc + mm(dsb, in_recv[2, ib * TB : (ib + 1) * TB], NN)
            q_acc[ib] = q_acc[ib] + mm(kt[:, jb * TB : (jb + 1) * TB], dsb, NN)
        g_send[3, jb * TB : (jb + 1) * TB] = acc.astype(jnp.bfloat16)
    sheared = []
    for m in range(nt):
        x = jnp.concatenate([diag[m], jnp.zeros((TB, TB), jnp.float32)], 1)
        size = TB
        while size > 8:
            size //= 2
            x = x[:size] + pltpu.roll(x[size:], 2 * TB - size, 1)
        for bit in (1, 2, 4):
            x = jnp.where((row8 & bit) != 0, pltpu.roll(x, 2 * TB - bit, 1), x)
        sheared.append(jnp.sum(x, axis=0, keepdims=True))
    by_distance = []
    for m in range(nt):
        part = sheared[m][:, :TB]
        if m + 1 < nt:
            part = part + sheared[m + 1][:, TB:]
        by_distance.append(part)
    by_distance = jnp.concatenate(by_distance, 1)
    db_col = jnp.sum(jnp.where(onehot, by_distance, 0.0), axis=1, keepdims=True)
    db_send[0] = jnp.sum(jnp.where(eye, db_col, 0.0), axis=0, keepdims=True)

    collects = c == 0
    in_own = jnp.logical_and(collects, own)

    def db_copy(m):
        return remote(db_send.at[0], db_recv.at[k], s_db.at[m], r_db.at[k], (m * H + head, 0))

    def db_each(action):
        for m in range(U // H):

            @pl.when(jnp.logical_not(jnp.logical_and(m * H + head == k, collects)))
            def _(m=m):
                action(db_copy(m))

    db_each(lambda copy: copy.start())

    @pl.when(in_own)
    def _():
        db_recv[k] = db_send[0]

    for jb in range(nt):
        acc = jnp.zeros((TB, W), jnp.float32)
        for ib in range(jb, nt):
            acc = acc + mm(wts[tile_at(ib, jb)], dat[:, ib * TB : (ib + 1) * TB], NT)
        g_send[1, jb * TB : (jb + 1) * TB] = acc.astype(jnp.bfloat16)
    for ib in range(nt):
        for p in range(per):
            r = ib * per + p
            g_send[2, r * W : (r + 1) * W] = (
                q_acc[ib][:, p * W : (p + 1) * W].T.astype(jnp.bfloat16)
            )
    for o in range(len(early) + 1, H):
        out_copy(o).start()

    half, most = H // 2, H - max(1, H // 4)
    for o in range(half):
        g_start(o)
    for o in range(half // 2):
        g_left(o)

    def dbs_copy(j):
        p = comp * H + j
        return remote(db_sum.at[0], db_mine.at[0], s_dbs.at[j], r_dbs, (p, ctx_of(e, p, H)))

    @pl.when(collects)
    def _():
        def db_wait(o):
            p = lax.rem(k + o, U)

            @pl.when(jnp.logical_not(jnp.logical_and(o == 0, in_own)))
            def _():
                arrived(db_recv.at[p], s_db.at[0], r_db.at[p])

        loop(0, U, db_wait)
        db_sum[0] = jnp.sum(db_recv[...], axis=0)
        for j in range(H):

            @pl.when(jnp.logical_not(jnp.logical_and(in_own, comp * H + j == k)))
            def _(j=j):
                dbs_copy(j).start()

    for o in range(half, most):
        g_start(o)
    for o in range(half // 2, half):
        g_left(o)

    @pl.when(in_own)
    def _():
        db_mine[0] = db_sum[0]

    @pl.when(jnp.logical_not(in_own))
    def _():
        arrived(db_mine.at[0], s_dbs.at[0], r_dbs)

    def dba_copy(o):
        cc = lax.rem(c + o, H)
        return remote(db_mine.at[0], db_all.at[c], s_dba.at[o], r_dba.at[c], (k, cc))

    loop(1, H, lambda o: dba_copy(o).start())
    db_all[c] = db_mine[0]

    for o in range(most, H):
        g_start(o)

    def dba_wait(o):
        cc = lax.rem(c + o, H)
        arrived(db_all.at[cc], s_dba.at[0], r_dba.at[cc])

    loop(1, H, dba_wait)

    def dba_put(cc):
        dbias[pl.ds(head_of(cc, k, H), 1), :] = db_all[cc]

    loop(0, H, dba_put)

    keep.wait()

    loop(0, U, lambda d: arrived(grads.at[d], s_g.at[0], r_g.at[d]))

    def ctx_end(o):
        cc = lax.rem(c + o, H)
        ref = out.at[:, rows(head_of(cc, k, H))]
        arrived(ref, s_out.at[0], r_out.at[cc])
        st_copy(o).wait_send()
        dba_copy(o).wait_send()
        cot_copy(o).wait_send()
        out_copy(o).wait_send()

    loop(1, H, ctx_end)

    @pl.when(jnp.logical_not(own))
    def _():
        in_copy(0).wait_send()

    loop(1, U, lambda o: in_copy(o).wait_send())
    for o in range(half, H):
        g_left(o)
    db_each(lambda copy: copy.wait_send())

    @pl.when(collects)
    def _():
        for j in range(H):

            @pl.when(jnp.logical_not(jnp.logical_and(in_own, comp * H + j == k)))
            def _(j=j):
                dbs_copy(j).wait_send()


def place(U, assign, out, grads, dbias, to_out, to_grads, to_bias, rows, blocks, bias, s_in, s_out):
    parts = 4
    some = U // parts

    def load(n):
        part = pl.ds(n * some, some)
        return pltpu.make_async_copy(grads.at[part], blocks.at[part], s_in.at[n])

    def store(d):
        return pltpu.make_async_copy(blocks.at[d], to_grads.at[assign[d]], s_out.at[d])

    ends = [(out, rows, to_out), (dbias, bias, to_bias)]
    first = [pltpu.make_async_copy(a, b, s_in.at[parts + n]) for n, (a, b, _) in enumerate(ends)]
    last = [pltpu.make_async_copy(b, c, s_out.at[U + n]) for n, (_, b, c) in enumerate(ends)]
    for n in range(parts):
        load(n).start()
    for copy in first:
        copy.start()
    for n in range(parts):
        load(n).wait()
        for d in range(n * some, (n + 1) * some):
            store(d).start()
    for a, b in zip(first, last):
        a.wait()
        b.start()
    for d in range(U):
        store(d).wait()
    for copy in last:
        copy.wait()


def on_device(uvqk, lengths, assignment, buckets, rel_bias, cotangent):
    U = assignment.shape[0]
    H = rel_bias.shape[0]
    LEN = buckets.shape[0]
    D = H * W
    nt = LEN // TB
    tiles = nt * (nt + 1) // 2
    vm = pl.BlockSpec(memory_space=pltpu.VMEM)
    hbm = pl.BlockSpec(memory_space=pltpu.HBM)
    bf, f32 = jnp.bfloat16, jnp.float32
    dma = pltpu.SemaphoreType.DMA
    shapes = [
        jax.ShapeDtypeStruct((W, D), bf),
        jax.ShapeDtypeStruct((U, W, W), bf),
        jax.ShapeDtypeStruct((H, W), f32),
    ]

    out, grads, dbias = pl.pallas_call(
        functools.partial(kernel, H, U),
        out_shape=shapes,
        in_specs=[hbm] * 6,
        out_specs=[hbm, hbm, vm],
        scratch_shapes=[
            pltpu.SMEM((U,), jnp.int32),
            pltpu.SMEM((U,), jnp.int32),
            pltpu.VMEM((U, W, W), bf),
            pltpu.VMEM((W, D), bf),
            pltpu.VMEM((1, LEN), jnp.int32),
            pltpu.VMEM((H, W), f32),
            pltpu.VMEM((U, W, W), bf),
            pltpu.VMEM((4, LEN, W), bf),
            pltpu.VMEM((LEN, W), bf),
            pltpu.VMEM((LEN, W), bf),
            pltpu.VMEM((4, LEN, W), bf),
            pltpu.VMEM((nt, TB, TB), f32),
            pltpu.VMEM((tiles, TB, TB), bf),
            pltpu.VMEM((tiles, TB, TB), f32),
            pltpu.VMEM((nt, TB, TB), f32),
            pltpu.VMEM((W, LEN), bf),
            pltpu.VMEM((W, LEN), bf),
            pltpu.VMEM((W, LEN), f32),
            pltpu.VMEM((W, LEN), f32),
            pltpu.VMEM((W, LEN), bf),
            pltpu.VMEM((H, 4, H, W), f32),
            pltpu.VMEM((4, H, W), f32),
            pltpu.VMEM((1, 1, W), f32),
            pltpu.VMEM((U, 1, W), f32),
            pltpu.VMEM((1, 1, W), f32),
            pltpu.VMEM((1, 1, W), f32),
            pltpu.VMEM((H, 1, W), f32),
            dma((6,)),
            dma((U,)),
            dma((4 * H,)),
            dma((H,)),
            dma((H,)),
            dma((H,)),
            dma((H,)),
            dma((H,)),
            dma((H,)),
            dma((4 * H,)),
            dma((U,)),
            dma((U // H,)),
            dma((U,)),
            dma((H,)),
            dma,
            dma((H,)),
            dma((H,)),
        ],
        compiler_params=pltpu.CompilerParams(
            collective_id=0, has_side_effects=True, vmem_limit_bytes=60 * 1024 * 1024
        ),
        name="layer",
    )(
        assignment,
        lengths,
        uvqk,
        cotangent.reshape(W, D),
        buckets.reshape(1, LEN),
        rel_bias,
    )
    out, grads, dbias = pl.pallas_call(
        functools.partial(place, U),
        out_shape=shapes,
        in_specs=[pl.BlockSpec(memory_space=pltpu.SMEM), hbm, hbm, hbm],
        out_specs=[hbm, hbm, hbm],
        scratch_shapes=[
            pltpu.VMEM((W, D), bf),
            pltpu.VMEM((U, W, W), bf),
            pltpu.VMEM((H, W), f32),
            dma((U + 2,)),
            dma((U + 2,)),
        ],
        compiler_params=pltpu.CompilerParams(vmem_limit_bytes=60 * 1024 * 1024),
        name="place",
    )(assignment, out, grads, dbias)
    return out.reshape(1, W, D), grads, dbias


def solution(mesh):
    in_specs = (P(None, "ctx", "dp"), P(), P(), P(), P(), P("dp", "ctx", None))
    out_specs = (P("dp", "ctx", None), P(None, "ctx", "dp"), P())
    return jax.shard_map(
        on_device, mesh=mesh, in_specs=in_specs, out_specs=out_specs, check_vma=False
    )
```

profile of v0, /device:TPU:1, one launch (start us, length us, event | category | flops | bytes accessed | tf_op | source)
XLA Modules:
  0.0 79.5 jit_solution(16222289353396913004)
XLA Ops:
  0.6 75.6 %layer.1 = (bf16[128,1024]{1,0:T(8,128)(2,1)}, bf16[32,128,128]{2,1,0:T(8,128)(2,1)}, f32[8,128]{1,0:T(8,128)}) custom-call(s32[32]{0:T(128)} %assign.1, s32[32]{0:T(128)} %lengths_hbm.1, bf16[32,128,128]{2,1,0:T(8,128)(2,1)} %uvqk_hbm.1, bf16[128,1024]{1,0:T(8,128)(2,1)} %bitcast.3, s32[1,1024]{1,0:T(1,128)} %bitcast.4, f32[8,128]{1,0:T(8,128)} %rel_hbm.1), custom_call_target="tpu_custom_call" | custom-call | tf_op jit(solution)/shard_map/layer/pallas_call | solution.py:601
  76.2 3.3 %place.1 = (bf16[128,1024]{1,0:T(8,128)(2,1)}, bf16[32,128,128]{2,1,0:T(8,128)(2,1)}, f32[8,128]{1,0:T(8,128)}) custom-call(s32[32]{0:T(128)} %assign.1, bf16[128,1024]{1,0:T(8,128)(2,1)} %get-tuple-element.9.out, bf16[32,128,128]{2,1,0:T(8,128)(2,1)} %get-tuple-element.10.grads, f32[8,128]{1,0:T(8,128)} %get-tuple-element.11.dbias), custom_call_target="tpu_custom_call" | custom-call | tf_op jit(solution)/shard_map/place/pallas_call | solution.py:664
where the time goes:
time: 79.9 us; the launch traced here: 79.5 us
  Pallas kernels  78.9 us (99%)
    pallas_call x1, Pallas kernels, on_device(): pl.pallas_call(functools.partial(kernel, H, U), out_shape=shapes, in_spec...  75.6 us
    pallas_call x1, Pallas kernels, on_device(): pl.pallas_call(functools.partial(place, U), out_shape=shapes, in_specs=[p...  3.26 us

commit v1 on v0

--- a/solution.py
+++ b/solution.py
@@ -48,13 +48,14 @@
     rel_hbm,
     out,
     grads,
-    dbias,
+    dbias_hbm,
     assign,
     lengths,
     uvqk,
     cot,
     buckets,
     rel,
+    dbias,
     in_send,
     in_recv,
     cot_recv,
@@ -340,7 +341,7 @@
             (which * H + head, cc),
         )
 
-    early = range(1, H // 2 + 1)
+    early = range(1, max(1, H // 4) + 1)
 
     def g_start(o):
         for n in range(4):
@@ -516,8 +517,11 @@
         dbias[pl.ds(head_of(cc, k, H), 1), :] = db_all[cc]
 
     loop(0, H, dba_put)
+    put = pltpu.make_async_copy(dbias, dbias_hbm, s_load.at[0])
+    put.start()
 
     keep.wait()
+    put.wait()
 
     loop(0, U, lambda d: arrived(grads.at[d], s_g.at[0], r_g.at[d]))
 
@@ -550,7 +554,9 @@
                 dbs_copy(j).wait_send()
 
 
-def place(U, assign, out, grads, dbias, to_out, to_grads, to_bias, rows, blocks, bias, s_in, s_out):
+def place(
+    U, users, out, grads, dbias, to_out, to_grads, to_bias, assign, rows, blocks, bias, s_in, s_out
+):
     parts = 4
     some = U // parts
 
@@ -564,10 +570,13 @@
     ends = [(out, rows, to_out), (dbias, bias, to_bias)]
     first = [pltpu.make_async_copy(a, b, s_in.at[parts + n]) for n, (a, b, _) in enumerate(ends)]
     last = [pltpu.make_async_copy(b, c, s_out.at[U + n]) for n, (_, b, c) in enumerate(ends)]
+    ids = pltpu.make_async_copy(users, assign, s_in.at[U])
+    ids.start()
     for n in range(parts):
         load(n).start()
     for copy in first:
         copy.start()
+    ids.wait()
     for n in range(parts):
         load(n).wait()
         for d in range(n * some, (n + 1) * some):
@@ -588,7 +597,6 @@
     D = H * W
     nt = LEN // TB
     tiles = nt * (nt + 1) // 2
-    vm = pl.BlockSpec(memory_space=pltpu.VMEM)
     hbm = pl.BlockSpec(memory_space=pltpu.HBM)
     bf, f32 = jnp.bfloat16, jnp.float32
     dma = pltpu.SemaphoreType.DMA
@@ -602,13 +610,14 @@
         functools.partial(kernel, H, U),
         out_shape=shapes,
         in_specs=[hbm] * 6,
-        out_specs=[hbm, hbm, vm],
+        out_specs=[hbm, hbm, hbm],
         scratch_shapes=[
             pltpu.SMEM((U,), jnp.int32),
             pltpu.SMEM((U,), jnp.int32),
             pltpu.VMEM((U, W, W), bf),
             pltpu.VMEM((W, D), bf),
             pltpu.VMEM((1, LEN), jnp.int32),
+            pltpu.VMEM((H, W), f32),
             pltpu.VMEM((H, W), f32),
             pltpu.VMEM((U, W, W), bf),
             pltpu.VMEM((4, LEN, W), bf),
@@ -664,9 +673,10 @@
     out, grads, dbias = pl.pallas_call(
         functools.partial(place, U),
         out_shape=shapes,
-        in_specs=[pl.BlockSpec(memory_space=pltpu.SMEM), hbm, hbm, hbm],
+        in_specs=[hbm] * 4,
         out_specs=[hbm, hbm, hbm],
         scratch_shapes=[
+            pltpu.SMEM((U,), jnp.int32),
             pltpu.VMEM((W, D), bf),
             pltpu.VMEM((U, W, W), bf),
             pltpu.VMEM((H, W), f32),

time: 79.9 us -> 78.2 us (0.979)
  Pallas kernels: 78.9 us -> 77 us
    pallas_call x1, Pallas kernels: 75.6 us -> 74.4 us  [on_device(): pl.pallas_call(functools.partial(kernel, H, U), out_shape=shapes, in_spec...]
where the time goes in v1:
time: 78.2 us; the launch traced here: 77.7 us
  Pallas kernels  77 us (98%)
    pallas_call x1, Pallas kernels, on_device(): pl.pallas_call(functools.partial(kernel, H, U), out_shape=shapes, in_spec...  74.4 us
    pallas_call x1, Pallas kernels, on_device(): pl.pallas_call(functools.partial(place, U), out_shape=shapes, in_specs=[h...  2.6 us

profile of v1, /device:TPU:1, one launch (start us, length us, event | category | flops | bytes accessed | tf_op | source)
XLA Modules:
  0.0 77.7 jit_solution(2684387838671296790)
XLA Ops:
  0.6 74.4 %layer.1 = (bf16[128,1024]{1,0:T(8,128)(2,1)}, bf16[32,128,128]{2,1,0:T(8,128)(2,1)}, f32[8,128]{1,0:T(8,128)}) custom-call(s32[32]{0:T(128)} %users.1, s32[32]{0:T(128)} %lengths_hbm.1, bf16[32,128,128]{2,1,0:T(8,128)(2,1)} %uvqk_hbm.1, bf16[128,1024]{1,0:T(8,128)(2,1)} %bitcast.3, s32[1,1024]{1,0:T(1,128)} %bitcast.4, f32[8,128]{1,0:T(8,128)} %rel_hbm.1), custom_call_target="tpu_custom_call" | custom-call | tf_op jit(solution)/shard_map/layer/pallas_call | solution.py:609
  75.1 2.6 %place.1 = (bf16[128,1024]{1,0:T(8,128)(2,1)}, bf16[32,128,128]{2,1,0:T(8,128)(2,1)}, f32[8,128]{1,0:T(8,128)}) custom-call(s32[32]{0:T(128)} %users.1, bf16[128,1024]{1,0:T(8,128)(2,1)} %get-tuple-element.9.out, bf16[32,128,128]{2,1,0:T(8,128)(2,1)} %get-tuple-element.10.grads, f32[8,128]{1,0:T(8,128)} %get-tuple-element.11.dbias), custom_call_target="tpu_custom_call" | custom-call | tf_op jit(solution)/shard_map/place/pallas_call | solution.py:673
